TPU v7x, 512 devices: a whole 4x4x16 slice. The times are simulated.
512 devices in a mesh: basin: 8 (over x, core), front: 64 (over y, z).
Axes of the slice: x: 4, y: 4, z: 16, core: 2. Of those that a mesh axis runs over, the one named last changes fastest.
Arguments:
- right_side: float32 [4, 8, 128, 512], P(None, 'basin', 'front'), may hold values from -8 to 8
- offsets: float32 [2, 8, 128, 512], P(None, 'basin', 'front'), may hold values from 0 to 1
- counts: int32 [8, 128], P('basin', 'front'), may hold values from 128 to 512, as said below
Outputs:
- solution_field: float32 [4, 8, 128, 512], P(None, 'basin', 'front')
- residual: float32 [4, 8, 128, 512], P(None, 'basin', 'front')
Inputs may be any that keep to these rules, and one draw needn't show every extreme that they name: Points p < counts of a block are live, the others are padding. Some block holds 512 live points, some 512 // 4.
All inputs are finite; a program needn't handle non-finite values.
Results may differ from a plain program's by a relative error of at most 0.0003.
Values sent between devices are 32-bit elements; how exact they have to be, the bound alone decides.
A program may use at most 64 MiB of HBM per device.

v0:
```python
from functools import partial

import jax
import jax.numpy as jnp
from jax import lax
from jax.sharding import PartitionSpec as P

ITERS = 3


ridge = 0.25
tile_rows = 128
all_neighbors = [(-1, -1), (-1, 0), (-1, 1), (0, -1), (0, 0), (0, 1), (1, -1), (1, 0), (1, 1)]


def with_halo(block, sides, width):
    for axis, dim in sides:
        count = lax.axis_size(axis)
        forward = [(i, i + 1) for i in range(count - 1)]
        backward = [(target, source) for source, target in forward]
        low = lax.ppermute(
            lax.slice_in_dim(block, block.shape[dim] - width, None, axis=dim), axis, forward
        )
        high = lax.ppermute(lax.slice_in_dim(block, 0, width, axis=dim), axis, backward)
        block = jnp.concatenate([low, block, high], axis=dim)
    return block


def wendland(delta_x, delta_y):
    radius = jnp.sqrt(delta_x * delta_x + delta_y * delta_y)
    near = jnp.maximum(1.0 - radius, 0.0)
    near_sq = near * near
    return near_sq * near_sq * (4.0 * radius + 1.0)


def expand(vector):
    return vector[:, None, None, None]


def flatten(block_grid):
    channels = block_grid.shape[0]
    points = block_grid.shape[3]
    return jnp.transpose(block_grid, (1, 2, 0, 3)).reshape(-1, channels, points)


def pair_terms(element, with_back):
    first_offs, second_offs, first_coef, second_coef, displace = element
    blocks, fields, points = second_coef.shape
    tile = min(tile_rows, points)
    tiles = points // tile
    first_x = jnp.transpose(first_offs[:, 0].reshape(blocks, tiles, tile), (1, 0, 2))
    first_y = jnp.transpose(first_offs[:, 1].reshape(blocks, tiles, tile), (1, 0, 2))
    first_tiles = jnp.transpose(first_coef.reshape(blocks, fields, tiles, tile), (2, 0, 1, 3))
    second_x = second_offs[:, 0][:, None, :] + displace[0]
    second_y = second_offs[:, 1][:, None, :] + displace[1]

    def tile_step(backward, parts):
        rows_x, rows_y, coef_tile = parts
        kernel = wendland(rows_x[:, :, None] - second_x, rows_y[:, :, None] - second_y)
        forward = jnp.einsum("bfj,bij->bfi", second_coef, kernel, precision=lax.Precision.HIGHEST)
        return (backward, forward)

    backward, forward = lax.scan(
        tile_step, jnp.zeros((blocks, fields, points), jnp.float32), (first_x, first_y, first_tiles)
    )
    forward = jnp.transpose(forward, (1, 2, 0, 3)).reshape(blocks, fields, points)
    return (forward, backward)


def stack_pairs(neighbor_list, direction, coef_pad, offs_pad):
    fields, rows_b, cols_b, points = direction.shape
    local_offs = flatten(offs_pad[:, 1 : rows_b + 1, 1 : cols_b + 1])
    local_coef = flatten(direction)
    first_offs, second_offs, first_coef, second_coef, displaces = ([], [], [], [], [])
    for row_step, col_step in neighbor_list:
        first_offs.append(local_offs)
        first_coef.append(local_coef)
        second_offs.append(
            flatten(
                offs_pad[
                    :, 1 + row_step : 1 + row_step + rows_b, 1 + col_step : 1 + col_step + cols_b
                ]
            )
        )
        second_coef.append(
            flatten(
                coef_pad[
                    :, 1 + row_step : 1 + row_step + rows_b, 1 + col_step : 1 + col_step + cols_b
                ]
            )
        )
        displaces.append(jnp.array([float(row_step), float(col_step)], jnp.float32))
    return (
        jnp.stack(first_offs),
        jnp.stack(second_offs),
        jnp.stack(first_coef),
        jnp.stack(second_coef),
        jnp.stack(displaces),
    )


def regrid(flat_terms, count, rows_b, cols_b):
    fields, points = (flat_terms.shape[-2], flat_terms.shape[-1])
    shaped = flat_terms.reshape(count, rows_b, cols_b, fields, points)
    return jnp.transpose(shaped, (0, 3, 1, 2, 4))


def operate(direction, offs_pad, live):
    fields, rows_b, cols_b, points = direction.shape
    coef_pad = with_halo(direction, (("basin", 1), ("front", 2)), 1)
    stacks = stack_pairs(all_neighbors, direction, coef_pad, offs_pad)
    forward, unused_back = lax.map(partial(pair_terms, with_back=False), stacks)
    summed = jnp.sum(regrid(forward, len(all_neighbors), rows_b, cols_b), axis=0)
    return ridge * direction + live * (summed / points)


def squares(residual):
    return lax.psum(jnp.sum(residual * residual, axis=(1, 2, 3)), ("basin", "front"))


def shards(right_side, offsets, counts):
    offs_pad = with_halo(offsets, (("basin", 1), ("front", 2)), 1)
    live = (lax.broadcasted_iota(jnp.int32, offsets.shape[1:], 2) < counts[:, :, None]).astype(
        jnp.float32
    )
    residual = right_side * live
    solution_field = jnp.zeros_like(residual)
    direction = residual
    norm_now = squares(residual)
    for repeat in range(ITERS):
        image = operate(direction, offs_pad, live)
        alpha = norm_now / lax.psum(jnp.sum(direction * image, axis=(1, 2, 3)), ("basin", "front"))
        solution_field = solution_field + expand(alpha) * direction
        residual = residual - expand(alpha) * image
        norm_next = squares(residual)
        direction = residual + expand(norm_next / norm_now) * direction
        norm_now = norm_next
    return (solution_field, residual)


def solution(mesh):
    in_specs = (
        P(None, "basin", "front", None),
        P(None, "basin", "front", None),
        P("basin", "front"),
    )
    out_specs = (P(None, "basin", "front", None), P(None, "basin", "front", None))
    return jax.shard_map(shards, mesh=mesh, in_specs=in_specs, out_specs=out_specs, check_vma=False)
```

profile of v0, /device:TPU:1, one launch (start us, length us, event | category | flops | bytes accessed | tf_op | source)
XLA Modules:
  0.0 740.9 jit_solution(9973013715917265255)
XLA Ops:
  2.1 4.5 collective-permute-start.4
  6.6 5.6 collective-permute-start.5
  16.6 2.5 collective-permute-done.1
  22.1 4.2 collective-permute-start.6
  27.8 3.2 collective-permute-done.7
  32.6 54.1 %while.61 = (s32[]{:T(128)}, f32[9,2,4,512]{3,2,1,0:T(4,128)S(1)}, f32[9,2,2,512]{3,1,2,0:T(2,128)S(1)}, f32[9,2,2,512]{3,1,2,0:T(2,128)S(1)}, f32[9,2]{0,1:T(2,...) while((s32[]{:T(128)}, f32[9,2,4,512]{3,2,1,0:T(4,128)S(1)}, ...), condition=%wide.region_5.6_spmd, body=%wide.region_2.5_spmd.sunk | while | flops 7866372 | bytes 248122 | solution.py:112
  34.6 3.8 while.66
  40.7 3.8 while.66
  46.7 3.8 while.66
  52.7 3.8 while.66
  58.7 3.8 while.66
  64.7 3.8 while.66
  70.7 3.8 while.66
  76.7 3.8 while.66
  82.7 3.8 while.66
  86.8 110.9 %all-reduce = (f32[4]{0:T(128)S(1)}, f32[4]{0:T(128)S(1)}) all-reduce(f32[4]{0:T(128)S(1)} %get-tuple-element.293, f32[4]{0:T(128)S(1)} %get-tuple-element.292), channel_id=1, replica_groups=mesh['basin'=8,'front'=64] {'basin','front'}, use_global_device_ids=true, to_apply=%region_1.0 | all-reduce | flops 8 | bytes 64 | tf_op jit(solution)/shard_map/psum | solution.py:118
  197.9 98.8 %psum.44 = f32[4]{0:T(128)S(1)} all-reduce(f32[4]{0:T(128)S(1)} %get-tuple-element.376), channel_id=1, replica_groups=mesh['basin'=8,'front'=64] {'basin','front'}, use_global_device_ids=true, to_apply=%region_10.11 | all-reduce | flops 4 | bytes 32 | tf_op jit(solution)/shard_map/psum | solution.py:118
  296.7 3.1 collective-permute-start.8
  301.8 3.1 collective-permute-done.9
  305.0 3.7 collective-permute-start.10
  310.0 3.2 collective-permute-done.11
  313.4 54.1 %while.63 = (s32[]{:T(128)}, f32[9,2,4,512]{3,2,1,0:T(4,128)S(1)}, f32[9,2,2,512]{3,1,2,0:T(2,128)S(1)}, f32[9,2,2,512]{3,1,2,0:T(2,128)S(1)}, f32[9,2]{0,1:T(2,...) while((s32[]{:T(128)}, f32[9,2,4,512]{3,2,1,0:T(4,128)S(1)}, ...), condition=%wide.region_14.15_spmd, body=%wide.region_11.14_spmd.sunk | while | flops 7866372 | bytes 248122 | solution.py:112
  315.5 3.8 while.67
  321.5 3.8 while.67
  327.5 3.8 while.67
  333.5 3.8 while.67
  339.5 3.8 while.67
  345.6 3.8 while.67
  351.6 3.8 while.67
  357.6 3.8 while.67
  363.6 3.8 while.67
  367.7 101.2 %psum.45 = f32[4]{0:T(128)S(1)} all-reduce(f32[4]{0:T(128)S(1)} %multiply_reduce_fusion.2), channel_id=1, replica_groups=mesh['basin'=8,'front'=64] {'basin','front'}, use_global_device_ids=true, to_apply=%region_17.18 | all-reduce | flops 4 | bytes 32 | tf_op jit(solution)/shard_map/psum | solution.py:132
  469.1 98.3 %psum.46 = f32[4]{0:T(128)S(1)} all-reduce(f32[4]{0:T(128)S(1)} %get-tuple-element.374), channel_id=1, replica_groups=mesh['basin'=8,'front'=64] {'basin','front'}, use_global_device_ids=true, to_apply=%region_19.20 | all-reduce | flops 4 | bytes 32 | tf_op jit(solution)/shard_map/psum | solution.py:118
  567.5 3.0 collective-permute-start.12
  572.5 3.1 collective-permute-done.13
  575.6 3.7 collective-permute-start.14
  580.7 3.2 collective-permute-done.15
  584.0 54.1 %while.65 = (s32[]{:T(128)}, f32[9,2,4,512]{3,2,1,0:T(4,128)S(1)}, f32[9,2,2,512]{3,1,2,0:T(2,128)S(1)}, f32[9,2,2,512]{3,1,2,0:T(2,128)S(1)}, f32[9,2]{0,1:T(2,...) while((s32[]{:T(128)}, f32[9,2,4,512]{3,2,1,0:T(4,128)S(1)}, ...), condition=%wide.region_23.24_spmd, body=%wide.region_20.23_spmd.sunk | while | flops 7866372 | bytes 248122 | solution.py:112
  586.1 3.8 while.68
  592.2 3.8 while.68
  598.2 3.8 while.68
  604.2 3.8 while.68
  610.2 3.8 while.68
  616.2 3.8 while.68
  622.2 3.8 while.68
  628.2 3.8 while.68
  634.2 3.8 while.68
  638.3 101.2 %psum.47 = f32[4]{0:T(128)S(1)} all-reduce(f32[4]{0:T(128)S(1)} %multiply_reduce_fusion), channel_id=1, replica_groups=mesh['basin'=8,'front'=64] {'basin','front'}, use_global_device_ids=true, to_apply=%region_26.27 | all-reduce | flops 4 | bytes 32 | tf_op jit(solution)/shard_map/psum | solution.py:132
  (636 shorter events, 179.9 us)
Async XLA Ops:
  0.6 0.7 copy-start.3
  1.4 10.8 %copy-start = (f32[2,1,2,512]{3,2,1,0:T(2,128)S(1)}, f32[2,1,2,512]{3,2,1,0:T(2,128)}, u32[]{:S(2)}) copy-start(f32[2,1,2,512]{3,2,1,0:T(2,128)} %param.43) | copy-start | bytes 24580
  2.1 20.0 %collective-permute-start.4 = (f32[4,1,2,512]{3,0,2,1:T(4,128)S(1)}, f32[4,1,2,512]{3,0,2,1:T(4,128)S(1)}, u32[]{:S(2)}, u32[]{:S(2)}) collective-permute-start(f32[4,1,2,512]{3,0,2,1:T(4,128)S(1)} %copy_multiply_fusion), channel_id=1, source_target_pairs={{0,64},{64,128},{128,192},{192,256},{256,320},{320,384},{384,448},... | collective-permute-start | bytes 49160 | tf_op jit(solution)/shard_map/ppermute | solution.py:21
  6.6 15.5 %collective-permute-start.5 = (f32[4,1,2,512]{3,0,2,1:T(4,128)S(1)}, f32[4,1,2,512]{3,0,2,1:T(4,128)S(1)}, u32[]{:S(2)}, u32[]{:S(2)}) collective-permute-start(f32[4,1,2,512]{3,0,2,1:T(4,128)S(1)} %copy_multiply_fusion), channel_id=1, source_target_pairs={{64,0},{128,64},{192,128},{256,192},{320,256},{384,320},{448,384},... | collective-permute-start | bytes 49160 | tf_op jit(solution)/shard_map/ppermute | solution.py:24
  12.2 4.4 collective-permute-start
  14.1 5.0 collective-permute-start.1
  19.1 8.5 %collective-permute-start.2 = (f32[2,3,1,512]{3,2,0,1:T(1,128)S(1)}, f32[2,3,1,512]{3,2,0,1:T(1,128)S(1)}, u32[]{:S(2)}, u32[]{:S(2)}) collective-permute-start(f32[2,3,1,512]{3,2,0,1:T(1,128)S(1)} %get-tuple-element.415), channel_id=1, source_target_pairs={{0,1},{1,2},{2,3},{3,4},{4,5},{5,6},{6,7},{7,8},{8,9},{9,10},{10,1... | collective-permute-start | bytes 36872 | tf_op jit(solution)/shard_map/ppermute | solution.py:21
  20.8 6.9 collective-permute-start.3
  22.1 5.7 collective-permute-start.6
  26.3 4.8 collective-permute-start.7
  31.1 0.7 copy-start.1
  31.9 0.7 copy-start.2
  296.7 5.1 collective-permute-start.8
  299.9 5.1 collective-permute-start.9
  305.0 5.0 collective-permute-start.10
  308.7 4.6 collective-permute-start.11
  567.5 5.0 collective-permute-start.12
  570.6 5.1 collective-permute-start.13
  575.6 5.0 collective-permute-start.14
  579.3 4.6 collective-permute-start.15
where the time goes:
time: 743 us; the launch traced here: 741 us
  blocking collectives  510 us (69%)
  matrix products  102 us (14%)
  starting transfers between devices  42.7 us (6%)
  other arithmetic  38.3 us (5%)
  local copies, waits for them, and re-layouts  25 us (3%)
  waiting for transfers between devices  18.4 us (2%)
    psum x3, blocking collectives, squares(): lax.psum(jnp.sum(residual * residual, axis=(1, 2, 3)), ('basin', 'front'))  308 us
    psum x2, blocking collectives, shards(): lax.psum(jnp.sum(direction * image, axis=(1, 2, 3)), ('basin', 'front'))  202 us
    dot_general x108, matrix products, tile_step(): jnp.einsum('bfj,bij->bfi', second_coef, kernel, precision=lax.Precision.H...  102 us
    add x27, other arithmetic, pair_terms(): second_y = second_offs[:, 1][:, None, :] + displace[1]  35.9 us
    ppermute x8, starting transfers between devices, with_halo(): lax.ppermute(lax.slice_in_dim(block, block.shape[dim] - width, None, axis...  25.7 us
    ppermute x8, waiting for transfers between devices, with_halo(): lax.ppermute(lax.slice_in_dim(block, 0, width, axis=dim), axis, backward)  18.4 us
    ppermute x8, starting transfers between devices, with_halo(): lax.ppermute(lax.slice_in_dim(block, 0, width, axis=dim), axis, backward)  17 us
    slice x27, local copies, waits for them, and re-layouts, pair_terms(): second_y = second_offs[:, 1][:, None, :] + displace[1]  15.8 us
  transfers between devices with their start and end apart: 16, of which 6 were waited for; matrix products, arithmetic and copies ran while one was open for 0% of the time, Pallas kernels for 0%

commit v1 on v0

v1 whole, which is shorter than its diff:
```python
import jax
import jax.numpy as jnp
from jax import lax
from jax.experimental import pallas as pl
from jax.experimental.pallas import tpu as pltpu
from jax.sharding import PartitionSpec as P

MESH = pl.DeviceIdType.MESH
F32, BF16 = jnp.float32, jnp.bfloat16
STEPS = 3
FIELDS = 4
POINTS = 512
RIDGE = 0.25
CHUNK = 256
Z_SIZE = 16

SIDES = ((1, 0), (-1, 0), (0, 1), (0, -1), (1, 1), (1, -1), (-1, 1), (-1, -1))


def wrap(value, count):
    return lax.rem(value + count, count)


def halves(kernel_values):
    high = kernel_values.astype(BF16)
    return high, (kernel_values - high.astype(F32)).astype(BF16)


def left_operand(vector):
    high = vector.astype(BF16).astype(F32)
    stacked = jnp.concatenate([high, vector - high, jnp.zeros((8, POINTS), F32)], axis=0)
    return stacked.astype(BF16)


def times(left, high, low):
    return jnp.dot(left, high, preferred_element_type=F32) + jnp.dot(left, low, preferred_element_type=F32)


def quarter_wendland(distance_sq):
    radius = pltpu.reciprocal(lax.rsqrt(distance_sq), approx=True)
    near = jnp.maximum(1.0 - radius, 0.0)
    near_sq = near * near
    return near_sq * near_sq * (radius + 0.25)


def joined(top, bottom):
    return jnp.concatenate([top[0:4] + top[4:8], bottom[0:4] + bottom[4:8]], axis=0)


def fold(values):
    part = values[:, 0:128]
    for lane in range(128, POINTS, 128):
        part = part + values[:, lane : lane + 128]
    return part[0:4] + part[4:8]


def kernel(
    sizes, right_ref, offs_ref, counts_ref, out_ref, res_ref,
    first, second, third, high, low, part, got_basin, got_z, got_y,
    halo_send, halo_recv, sum_send, sum_recv,
):
    n_basin, n_front, n_y, n_z = sizes
    basin, front = lax.axis_index("basin"), lax.axis_index("front")
    y_at, z_at = front // n_z, lax.rem(front, n_z)

    def basin_peer(step):
        return (wrap(basin + step, n_basin), front)

    def z_peer(step):
        return (basin, y_at * n_z + wrap(z_at + step, n_z))

    def y_peer(step):
        return (basin, wrap(y_at + step, n_y) * n_z + z_at)

    def side_peer(side):
        return (wrap(basin + side[0], n_basin), wrap(front + side[1], n_front))

    groups = ((basin_peer, n_basin, got_basin), (z_peer, n_z, got_z), (y_peer, n_y, got_y))

    barrier = pltpu.get_barrier_semaphore()
    greeted = [peer(step) for peer, count, _ in groups for step in range(1, count)]
    greeted += [side_peer(side) for side in SIDES if side[1] != 0]
    for device in greeted:
        pl.semaphore_signal(barrier, inc=1, device_id=device, device_id_type=MESH)

    lane = lax.broadcasted_iota(jnp.int32, (FIELDS, POINTS), 1)
    alive = [(lane < counts_ref[0, block]).astype(F32) for block in range(2)]
    live = jnp.concatenate(alive, axis=0)
    residual = []
    for block in range(2):
        field = right_ref[:, 0, block, :] * alive[block]
        residual.append(field)
        first[5 + block] = jnp.concatenate(
            [field, offs_ref[:, 0, block, :], jnp.zeros((2, POINTS), F32)], axis=0
        )
    residual = jnp.concatenate(residual, axis=0)

    pl.semaphore_wait(barrier, len(greeted))

    def halo_copy(buffer, turn, index):
        row, col = SIDES[index]
        target = 1 - row
        if col == 0:
            source, dest = pl.ds(5, 2), pl.ds(4 * target + 1, 2)
        elif col == 1:
            source, dest = pl.ds(6, 1), pl.ds(4 * target, 1)
        else:
            source, dest = pl.ds(5, 1), pl.ds(4 * target + 3, 1)
        return pltpu.make_async_remote_copy(
            src_ref=buffer.at[source], dst_ref=buffer.at[dest],
            send_sem=halo_send.at[turn, index], recv_sem=halo_recv.at[turn, index],
            device_id=side_peer(SIDES[index]), device_id_type=MESH,
        )

    def halo_start(buffer, turn):
        copies = [halo_copy(buffer, turn, index) for index in range(8)]
        for copy in copies:
            copy.start()
        return copies

    copies = halo_start(first, 0)

    arrivals = {0: (0, (4, 5)), 1: (None, (2, 3)), 2: (1, (6, 7))}

    def far(row, col):
        outside = jnp.float32(0.0)
        if row == 0:
            outside = outside + (basin == 0).astype(F32)
        if row == 2:
            outside = outside + (basin == n_basin - 1).astype(F32)
        if col == 0:
            outside = outside + (front == 0).astype(F32)
        if col == 3:
            outside = outside + (front == n_front - 1).astype(F32)
        return outside * 64.0

    own_x = [first[5 + block, 4:5, :] for block in range(2)]
    own_y = [first[5, 5:6, :], first[6, 5:6, :] + 1.0]

    def users(col):
        return [block for block in range(2) if 0 <= col - block <= 2]

    def slot(block, row, col):
        return 9 * block + 3 * row + col - block

    zero = jnp.zeros((16, POINTS), F32)

    def build(row, cols, sums):
        for col in cols:
            packed = first[4 * row + col]
            columns = jnp.transpose(packed)
            at_x = columns[:, 4:5] + (float(row - 1) + far(row, col))
            at_y = columns[:, 5:6] + float(col - 1)
            left = left_operand(packed[0:4])
            for begin in range(0, POINTS, CHUNK):
                rows = slice(begin, begin + CHUNK)
                for block in users(col):
                    delta_x = own_x[block] - at_x[rows]
                    delta_y = own_y[block] - at_y[rows]
                    top, rest = halves(quarter_wendland(delta_x * delta_x + delta_y * delta_y))
                    place = slot(block, row, col)
                    high[place, rows, :] = top
                    low[place, rows, :] = rest
                    sums[block] = sums[block] + times(left[:, rows], top, rest)
        return sums

    def use(buffer, row, cols, sums):
        for col in cols:
            left = left_operand(buffer[4 * row + col])
            for block in users(col):
                place = slot(block, row, col)
                sums[block] = sums[block] + times(left, high[place], low[place])
        return sums

    def product(work, copies, between):
        sums = [zero, zero]
        for row in (1, 0, 2):
            middle, outer = arrivals[row]
            if middle is not None:
                copies[middle].wait_recv()
            sums = work(row, (1, 2), sums)
            for index in outer:
                copies[index].wait_recv()
            sums = work(row, (0, 3), sums)
            between(row)
        return joined(*sums) * (live * (4.0 / POINTS))

    def stage_all(turn, stage):
        got = groups[stage][2]
        return pltpu.make_async_remote_copy(
            src_ref=got.at[turn], dst_ref=got.at[turn],
            send_sem=sum_send.at[turn, stage], recv_sem=sum_recv.at[turn, stage],
            device_id=groups[stage][0](1), device_id_type=MESH,
        )

    def stage_start(turn, stage, value):
        part[turn, stage] = value
        peer, count, got = groups[stage]
        for step in range(1, count):
            pltpu.make_async_remote_copy(
                src_ref=part.at[turn, stage], dst_ref=got.at[turn, step - 1],
                send_sem=sum_send.at[turn, stage], recv_sem=sum_recv.at[turn, stage],
                device_id=peer(step), device_id_type=MESH,
            ).start()

    def stage_end(turn, stage):
        stage_all(turn, stage).wait_recv()
        return part[turn, stage] + jnp.sum(groups[stage][2][turn], axis=0)

    def sum_start(turn, residual, image):
        stage_start(
            turn, 0,
            jnp.concatenate([fold(residual * residual), fold(residual * image)], axis=0),
        )

    def sum_step(turn, stage):
        stage_start(turn, stage + 1, stage_end(turn, stage))

    def sum_end(turn):
        total = jnp.sum(stage_end(turn, 2), axis=1, keepdims=True)
        norm, curve = total[0:4], total[4:8]
        return jnp.concatenate([norm, norm], axis=0), jnp.concatenate([curve, curve], axis=0)

    buffers = (first, second, third)
    image = product(build, copies, lambda row: None)
    all_copies = [copies]
    found = jnp.zeros((2 * FIELDS, POINTS), F32)
    for turn in range(STEPS):
        last = turn == STEPS - 1
        if not last:
            buffer = buffers[turn + 1]
            buffer[5] = image[0:4]
            buffer[6] = image[4:8]
            copies = halo_start(buffer, turn + 1)
            all_copies.append(copies)
        sum_start(turn, residual, image)
        if not last:

            def between(row, turn=turn):
                if row == 1:
                    sum_step(turn, 0)
                if row == 0:
                    sum_step(turn, 1)

            image_next = product(lambda row, cols, sums: use(buffer, row, cols, sums), copies, between)
        else:
            sum_step(turn, 0)
            sum_step(turn, 1)
        norm, curve = sum_end(turn)
        curve = RIDGE * norm + curve
        if turn == 0:
            alpha = norm / curve
            direction, mapped = residual, image
            if not last:
                mapped_twice = image_next
        else:
            beta = norm / norm_before
            alpha = norm / (curve - beta * norm / alpha)
            direction = residual + beta * direction
            mapped = image + beta * mapped
            if not last:
                mapped_twice = image_next + beta * mapped_twice
        found = found + alpha * direction
        residual = residual - alpha * (RIDGE * direction + mapped)
        if not last:
            image = image - alpha * (RIDGE * mapped + mapped_twice)
        norm_before = norm

    for block in range(2):
        out_ref[:, 0, block, :] = found[4 * block : 4 * block + 4]
        res_ref[:, 0, block, :] = residual[4 * block : 4 * block + 4]

    for copies in all_copies:
        for copy in copies:
            copy.wait_send()
    for turn in range(STEPS):
        for stage in range(3):
            stage_all(turn, stage).wait_send()


def solution(mesh):
    n_basin, n_front = mesh.shape["basin"], mesh.shape["front"]
    n_z = Z_SIZE
    sizes = (n_basin, n_front, n_front // n_z, n_z)

    def step(right_side, offsets, counts):
        shape = jax.ShapeDtypeStruct(right_side.shape, F32)
        return pl.pallas_call(
            lambda *refs: kernel(sizes, *refs),
            out_shape=(shape, shape),
            in_specs=[
                pl.BlockSpec(memory_space=pltpu.VMEM),
                pl.BlockSpec(memory_space=pltpu.VMEM),
                pl.BlockSpec(memory_space=pltpu.SMEM),
            ],
            out_specs=(pl.BlockSpec(memory_space=pltpu.VMEM), pl.BlockSpec(memory_space=pltpu.VMEM)),
            scratch_shapes=[
                pltpu.VMEM((12, 8, POINTS), F32),
                pltpu.VMEM((12, FIELDS, POINTS), F32),
                pltpu.VMEM((12, FIELDS, POINTS), F32),
                pltpu.VMEM((18, POINTS, POINTS), BF16),
                pltpu.VMEM((18, POINTS, POINTS), BF16),
                pltpu.VMEM((STEPS, 3, 8, 128), F32),
                pltpu.VMEM((STEPS, n_basin - 1, 8, 128), F32),
                pltpu.VMEM((STEPS, n_z - 1, 8, 128), F32),
                pltpu.VMEM((STEPS, n_front // n_z - 1, 8, 128), F32),
                pltpu.SemaphoreType.DMA((STEPS, 8)),
                pltpu.SemaphoreType.DMA((STEPS, 8)),
                pltpu.SemaphoreType.DMA((STEPS, 3)),
                pltpu.SemaphoreType.DMA((STEPS, 3)),
            ],
            compiler_params=pltpu.CompilerParams(
                collective_id=0, has_side_effects=True, vmem_limit_bytes=48 * 2**20
            ),
        )(right_side, offsets, counts)

    part = P(None, "basin", "front", None)
    return jax.shard_map(
        step, mesh=mesh, in_specs=(part, part, P("basin", "front")), out_specs=(part, part), check_vma=False
    )
```

time: 743 us -> 81.3 us (0.11)
  blocking collectives: 510 us -> 0 us
  matrix products: 102 us -> 0 us
  Pallas kernels: 0 us -> 77.2 us
  starting transfers between devices: 42.7 us -> 0 us
  other arithmetic: 38.3 us -> 0 us
  local copies, waits for them, and re-layouts: 25 us -> 3.27 us
  waiting for transfers between devices: 18.4 us -> 0 us
    psum x5 -> x0, blocking collectives: 510 us -> none  [the longest x3 308 us: squares(): lax.psum(jnp.sum(residual * residual, axis=(1, 2, 3)), ('basin', 'front'))]
    dot_general x108 -> x0, matrix products: 102 us -> none  [tile_step(): jnp.einsum('bfj,bij->bfi', second_coef, kernel, precision=lax.Precision.H...]
    pallas_call x0 -> x1, Pallas kernels: none -> 77.2 us  [step(): pl.pallas_call(lambda *refs: kernel(sizes, *refs), out_shape=(shape, shap...]
    ppermute x16 -> x0, starting transfers between devices: 42.7 us -> none  [the longest x8 25.7 us: with_halo(): lax.ppermute(lax.slice_in_dim(block, block.shape[dim] - width, None, axis...]
    add x29 -> x0, other arithmetic: 36 us -> none  [the longest x27 35.9 us: pair_terms(): second_y = second_offs[:, 1][:, None, :] + displace[1]]
    ppermute x16 -> x0, waiting for transfers between devices: 18.4 us -> none  [the longest x8 18.4 us: with_halo(): lax.ppermute(lax.slice_in_dim(block, 0, width, axis=dim), axis, backward)]
    slice x58 -> x0, local copies, waits for them, and re-layouts: 15.9 us -> none  [the longest x27 15.8 us: pair_terms(): second_y = second_offs[:, 1][:, None, :] + displace[1]]
  transfers between devices with their start and end apart: 16 -> 0, of which waited for: 6 -> 0; matrix products, arithmetic and copies ran while one was open for 0% -> 0% of each run, Pallas kernels for 0% -> 0%
where the time goes in v1:
time: 81.3 us; the launch traced here: 81.1 us
  Pallas kernels  77.2 us (95%)
  local copies, waits for them, and re-layouts  3.27 us (4%)
    pallas_call x1, Pallas kernels, step(): pl.pallas_call(lambda *refs: kernel(sizes, *refs), out_shape=(shape, shap...  77.2 us
    unnamed x8, local copies, waits for them, and re-layouts  3.27 us

profile of v1, /device:TPU:1, one launch (start us, length us, event | category | flops | bytes accessed | tf_op | source)
XLA Modules:
  0.0 81.1 jit_solution(3630628696463052457)
XLA Ops:
  0.6 0.0 copy-start
  0.6 0.7 copy-done
  1.3 0.0 copy-start.1
  1.4 0.7 copy-done.1
  2.0 0.0 copy-start.2
  2.0 0.7 copy-done.2
  2.7 77.2 %shard_map.50 = (f32[4,1,2,512]{3,2,1,0:T(2,128)S(1)}, f32[4,1,2,512]{3,2,1,0:T(2,128)S(1)}) custom-call(f32[4,1,2,512]{3,2,1,0:T(2,128)S(1)} %copy-done, f32[2,1,2,512]{3,2,1,0:T(2,128)S(1)} %copy-done.1, s32[1,2]{1,0:T(1,128)S(1)} %copy-done.2), custom_call_target="tpu_custom_call" | custom-call | tf_op jit(solution)/shard_map/pallas_call | solution.py:288
  79.9 0.6 copy.7
  80.5 0.6 copy.8
Async XLA Ops:
  0.6 0.7 copy-start
  1.3 0.7 copy-start.1
  2.0 0.7 copy-start.2

commit v2 on v1

v2 whole, which is shorter than its diff:
```python
import jax
import jax.numpy as jnp
from jax import lax
from jax.experimental import pallas as pl
from jax.experimental.pallas import tpu as pltpu
from jax.sharding import PartitionSpec as P

MESH = pl.DeviceIdType.MESH
F32, BF16 = jnp.float32, jnp.bfloat16
FIELDS = 4
POINTS = 512
RIDGE = 0.25
CHUNK = 256
Z_SIZE = 16

SIDES = ((1, 0), (-1, 0), (0, 1), (0, -1), (1, 1), (1, -1), (-1, 1), (-1, -1))
ARRIVALS = ((0, (1, 2)), (2, (1, 2)), (1, (0,)), (1, (3,)), (0, (0,)), (0, (3,)), (2, (0,)), (2, (3,)))
ORDER = (0, 2, 4, 5, 1, 3, 6, 7)
SEND_ORDER = (4, 5, 0, 2, 6, 7, 1, 3)


def wrap(value, count):
    return lax.rem(value + count, count)


def halves(kernel_values):
    high = kernel_values.astype(BF16)
    return high, (kernel_values - high.astype(F32)).astype(BF16)


def left_operand(vector):
    high = vector.astype(BF16).astype(F32)
    rest = vector - high
    middle = rest.astype(BF16).astype(F32)
    stacked = jnp.concatenate([high, middle, rest - middle, jnp.zeros((4, POINTS), F32)], axis=0)
    return stacked.astype(BF16)


def times(left, high, low):
    return jnp.dot(left, high, preferred_element_type=F32) + jnp.dot(left, low, preferred_element_type=F32)


def quarter_wendland(distance_sq):
    radius = pltpu.reciprocal(lax.rsqrt(distance_sq), approx=True)
    near = jnp.maximum(1.0 - radius, 0.0)
    near_sq = near * near
    return near_sq * near_sq * (radius + 0.25)


def two_sum(a, b):
    total = a + b
    other = total - a
    return total, (a - (total - other)) + (b - other)


def quick_sum(a, b):
    total = a + b
    return total, b - (total - a)


def split(a):
    scaled = a * 4097.0
    high = scaled - (scaled - a)
    return high, a - high


def two_product(a, b):
    total = a * b
    a_high, a_low = split(a)
    b_high, b_low = split(b)
    return total, ((a_high * b_high - total) + a_high * b_low + a_low * b_high) + a_low * b_low


def minus(a, b):
    total, rest = two_sum(a[0], -b[0])
    return quick_sum(total, rest + (a[1] - b[1]))


def product_of(a, b):
    total, rest = two_product(a[0], b[0])
    return quick_sum(total, rest + (a[0] * b[1] + a[1] * b[0]))


def ratio(a, b):
    first = a[0] / b[0]
    left = minus(a, product_of(b, (first, jnp.zeros_like(first))))
    return quick_sum(first, (left[0] + left[1]) / b[0])


def coefficients(moments):
    a0 = ratio(moments[1], moments[0])
    one = [None] + [minus(moments[k + 1], product_of(a0, moments[k])) for k in range(1, 5)]
    mean_one = ratio(one[2], one[1])
    a1 = minus(mean_one, a0)
    b1 = ratio(one[1], moments[0])
    two = [
        minus(minus(one[k + 1], product_of(a1, one[k])), product_of(b1, moments[k])) for k in (2, 3)
    ]
    a2 = two[1][0] / two[0][0] - mean_one[0]
    b2 = two[0][0] / one[1][0]
    a0, a1, b1 = a0[0], a1[0], b1[0]
    constant, linear = a0 * a1 - b1, -(a0 + a1)
    c2, c1, c0 = linear - a2, constant - a2 * linear - b2, b2 * a0 - a2 * constant
    at_ridge = ((c2 - RIDGE) * -RIDGE + c1) * -RIDGE + c0
    d3 = 1.0 / at_ridge
    d2, d1, d0 = c2 * d3, c1 * d3, c0 * d3
    x2 = -d3
    x1 = -d2 - RIDGE * x2
    x0 = -d1 - RIDGE * x1
    return (x0, x1, x2), (d0, d1, d2, d3)


def joined(top, bottom):
    return jnp.concatenate([x[0:4] + (x[4:8] + x[8:12]) for x in (top, bottom)], axis=0)


def fold(values):
    part = values[:, 0:128]
    for lane in range(128, POINTS, 128):
        part = part + values[:, lane : lane + 128]
    return part[0:4] + part[4:8]


def kernel(
    sizes, right_hbm, offs_hbm, counts_hbm, out_ref, res_ref,
    right_ref, offs_ref, counts_ref, first, second, third, high, low, part, got_core, got_xy, got_z,
    load_sem, halo_send, halo_recv, sum_send, sum_recv,
):
    n_x, n_y, n_z = sizes
    n_basin, n_front = 2 * n_x, n_y * n_z
    basin, front = lax.axis_index("basin"), lax.axis_index("front")
    x_at, core_at = basin // 2, lax.rem(basin, 2)
    y_at, z_at = front // n_z, lax.rem(front, n_z)

    loads = [
        pltpu.make_async_copy(source, dest, load_sem.at[index])
        for index, (source, dest) in enumerate(
            ((right_hbm, right_ref), (offs_hbm, offs_ref), (counts_hbm, counts_ref))
        )
    ]
    for load in loads:
        load.start()

    def hops(step, count):
        return min(step, count - step)

    def xy_peer(step_x, step_y):
        return (2 * wrap(x_at + step_x, n_x) + core_at, wrap(y_at + step_y, n_y) * n_z + z_at)

    def side_peer(side):
        return (wrap(basin + side[0], n_basin), wrap(front + side[1], n_front))

    xy_steps = [(x, y) for x in range(n_x) for y in range(n_y) if x or y]
    xy_steps.sort(key=lambda step: -hops(step[0], n_x) - hops(step[1], n_y))
    z_steps = sorted(range(1, n_z), key=lambda step: -hops(step, n_z))
    stages = (
        ([(2 * x_at + 1 - core_at, front)], got_core),
        ([xy_peer(*step) for step in xy_steps], got_xy),
        ([(basin, y_at * n_z + wrap(z_at + step, n_z)) for step in z_steps], got_z),
    )

    barrier = pltpu.get_barrier_semaphore()
    greeted = [side_peer(side) for side in SIDES]
    for peers, _ in stages:
        greeted += peers
    for device in greeted:
        pl.semaphore_signal(barrier, inc=1, device_id=device, device_id_type=MESH)

    for load in loads:
        load.wait()
    lane = lax.broadcasted_iota(jnp.int32, (FIELDS, POINTS), 1)
    alive, residual = [], []
    for block in range(2):
        alive.append((lane < counts_ref[0:1, block : block + 1]).astype(F32))
        field = right_ref[:, 0, block, :] * alive[block]
        residual.append(field)
        first[5 + block] = jnp.concatenate(
            [field, offs_ref[:, 0, block, :], jnp.zeros((2, POINTS), F32)], axis=0
        )
    scale = jnp.concatenate(alive, axis=0) * (4.0 / POINTS)
    residual = jnp.concatenate(residual, axis=0)

    pl.semaphore_wait(barrier, len(greeted))

    def halo_start(buffer, turn):
        copies = []
        for index, (row, col) in enumerate(SIDES):
            target = 1 - row
            if col == 0:
                source, dest = pl.ds(5, 2), pl.ds(4 * target + 1, 2)
            elif col == 1:
                source, dest = pl.ds(6, 1), pl.ds(4 * target, 1)
            else:
                source, dest = pl.ds(5, 1), pl.ds(4 * target + 3, 1)
            copies.append(
                pltpu.make_async_remote_copy(
                    src_ref=buffer.at[source], dst_ref=buffer.at[dest],
                    send_sem=halo_send.at[turn, index], recv_sem=halo_recv.at[turn, index],
                    device_id=side_peer((row, col)), device_id_type=MESH,
                )
            )
        for index in SEND_ORDER:
            copies[index].start()
        return copies

    def far(row, col):
        outside = jnp.float32(0.0)
        if row == 0:
            outside = outside + (basin == 0).astype(F32)
        if row == 2:
            outside = outside + (basin == n_basin - 1).astype(F32)
        if col == 0:
            outside = outside + (front == 0).astype(F32)
        if col == 3:
            outside = outside + (front == n_front - 1).astype(F32)
        return outside * 64.0

    def users(col):
        return [block for block in range(2) if 0 <= col - block <= 2]

    def slot(block, row, col):
        return 9 * block + 3 * row + col - block

    zero = jnp.zeros((16, POINTS), F32)

    def build(row, cols, sums):
        sums = list(sums)
        for col in cols:
            packed = first[4 * row + col]
            columns = jnp.transpose(packed)
            at_x = columns[:, 4:5] + (float(row - 1) + far(row, col))
            at_y = columns[:, 5:6] + float(col - 1)
            left = left_operand(packed[0:4])
            for begin in range(0, POINTS, CHUNK):
                rows = slice(begin, begin + CHUNK)
                for block in users(col):
                    delta_x = own_x[block] - at_x[rows]
                    delta_y = own_y[block] - at_y[rows]
                    top, rest = halves(quarter_wendland(delta_x * delta_x + delta_y * delta_y))
                    place = slot(block, row, col)
                    high[place, rows, :] = top
                    low[place, rows, :] = rest
                    sums[block] = sums[block] + times(left[:, rows], top, rest)
        return sums

    def use(buffer, row, cols, sums):
        sums = list(sums)
        for col in cols:
            left = left_operand(buffer[4 * row + col])
            for block in users(col):
                place = slot(block, row, col)
                sums[block] = sums[block] + times(left, high[place], low[place])
        return sums

    def gather(work, copies, indices, sums):
        for index in indices:
            copies[index].wait_recv()
            sums = work(*ARRIVALS[index], sums)
        return sums

    row_at = lax.broadcasted_iota(jnp.int32, (8, 128), 0)
    lane_at = lax.broadcasted_iota(jnp.int32, (8, 128), 1)

    def own_moment(order, a, b):
        total = jnp.sum(fold(a * b), axis=1, keepdims=True)
        return jnp.where(lane_at[0:4] == row_at[0:4] + FIELDS * order, total, 0.0)

    def sum_copy(stage, index, peer):
        got = stages[stage][1]
        return pltpu.make_async_remote_copy(
            src_ref=part.at[pl.ds(stage, 1)], dst_ref=got.at[pl.ds(index, 1)],
            send_sem=sum_send.at[stage], recv_sem=sum_recv.at[stage],
            device_id=peer, device_id_type=MESH,
        )

    def sum_all(stage):
        peers, got = stages[stage]
        return pltpu.make_async_remote_copy(
            src_ref=got.at[pl.ds(0, len(peers))], dst_ref=got.at[pl.ds(0, len(peers))],
            send_sem=sum_send.at[stage], recv_sem=sum_recv.at[stage],
            device_id=peers[0], device_id_type=MESH,
        )

    def sum_start(stage, total, rest):
        peers, got = stages[stage]
        row = total if rest is None else jnp.where(lane_at[0:1] < 64, total, pltpu.roll(rest, 64, 1))
        part[stage : stage + 1] = row
        for index, peer in enumerate(peers):
            sum_copy(stage, index, peer).start()
        got[len(peers) : len(peers) + 1] = row

    def sum_end(stage):
        peers, got = stages[stage]
        sum_all(stage).wait_recv()
        count = len(peers) + 1
        if count < 8:
            total, rest = got[0:1], jnp.zeros((1, 128), F32)
            for index in range(1, count):
                total, more = two_sum(total, got[index : index + 1])
                rest = rest + more
        else:
            total, rest = got[0:8], jnp.zeros((8, 128), F32)
            for begin in range(8, count, 8):
                total, more = two_sum(total, got[begin : begin + 8])
                rest = rest + more
            for step in (4, 2, 1):
                total, more = two_sum(total, pltpu.roll(total, step, 0))
                rest = rest + pltpu.roll(rest, step, 0) + more
            total, rest = total[0:1], rest[0:1]
        return total, rest + pltpu.roll(total, 64, 1)

    copies = halo_start(first, 0)
    all_copies = [copies]
    own_x = [first[5 + block, 4:5, :] for block in range(2)]
    own_y = [first[5, 5:6, :], first[6, 5:6, :] + 1.0]
    sums = build(1, (1, 2), [zero, zero])
    sums = gather(build, copies, ORDER, sums)
    powers = [residual, joined(*sums) * scale]

    def send(buffer, turn):
        buffer[5] = powers[-1][0:4]
        buffer[6] = powers[-1][4:8]
        all_copies.append(halo_start(buffer, turn))
        return all_copies[-1], lambda row, cols, sums: use(buffer, row, cols, sums)

    copies, work = send(second, 1)
    moments = own_moment(0, powers[0], powers[0]) + own_moment(1, powers[0], powers[1])
    moments = moments + own_moment(2, powers[1], powers[1])
    sums = work(1, (1, 2), [zero, zero])
    sums = gather(work, copies, ORDER, sums)
    powers.append(joined(*sums) * scale)

    copies, work = send(third, 2)
    moments = moments + own_moment(3, powers[1], powers[2]) + own_moment(4, powers[2], powers[2])
    own = work(1, (1, 2), [zero, zero])
    sums = gather(work, copies, ORDER[:4], [zero, zero])
    half = joined(*[a + 2.0 * b for a, b in zip(own, sums)]) * scale
    moments = jnp.sum(moments + own_moment(5, powers[2], half), axis=0, keepdims=True)
    sum_start(0, moments, None)
    sums = [a + b for a, b in zip(own, sums)]
    total, rest = sum_end(0)
    sum_start(1, total, rest)
    sums = gather(work, copies, ORDER[4:], sums)
    powers.append(joined(*sums) * scale)
    total, rest = sum_end(1)
    sum_start(2, total, rest)
    total, rest = sum_end(2)
    total, rest = quick_sum(total, rest)

    def moment(order):
        here = lane_at == lax.rem(row_at, FIELDS) + FIELDS * order
        return tuple(jnp.sum(jnp.where(here, value, 0.0), axis=1, keepdims=True) for value in (total, rest))

    found_by, left_by = coefficients([moment(order) for order in range(6)])

    def mix(factors):
        terms = [factor * power for factor, power in zip(factors, powers)]
        return sum(terms[1:], terms[0])

    found, left = mix(found_by), mix(left_by)
    for block in range(2):
        out_ref[:, 0, block, :] = found[4 * block : 4 * block + 4]
        res_ref[:, 0, block, :] = left[4 * block : 4 * block + 4]

    for copies in all_copies:
        for copy in copies:
            copy.wait_send()
    for stage in range(3):
        sum_all(stage).wait_send()


def solution(mesh):
    n_basin, n_front = mesh.shape["basin"], mesh.shape["front"]
    sizes = (n_basin // 2, n_front // Z_SIZE, Z_SIZE)
    n_xy = sizes[0] * sizes[1]

    def step(right_side, offsets, counts):
        shape = jax.ShapeDtypeStruct(right_side.shape, F32)
        return pl.pallas_call(
            lambda *refs: kernel(sizes, *refs),
            out_shape=(shape, shape),
            in_specs=[pl.BlockSpec(memory_space=pl.ANY)] * 3,
            out_specs=(pl.BlockSpec(memory_space=pltpu.VMEM), pl.BlockSpec(memory_space=pltpu.VMEM)),
            scratch_shapes=[
                pltpu.VMEM(right_side.shape, F32),
                pltpu.VMEM(offsets.shape, F32),
                pltpu.VMEM(counts.shape, jnp.int32),
                pltpu.VMEM((12, 8, POINTS), F32),
                pltpu.VMEM((12, FIELDS, POINTS), F32),
                pltpu.VMEM((12, FIELDS, POINTS), F32),
                pltpu.VMEM((18, POINTS, POINTS), BF16),
                pltpu.VMEM((18, POINTS, POINTS), BF16),
                pltpu.VMEM((3, 128), F32),
                pltpu.VMEM((2, 128), F32),
                pltpu.VMEM((n_xy, 128), F32),
                pltpu.VMEM((Z_SIZE, 128), F32),
                pltpu.SemaphoreType.DMA((3,)),
                pltpu.SemaphoreType.DMA((3, 8)),
                pltpu.SemaphoreType.DMA((3, 8)),
                pltpu.SemaphoreType.DMA((3,)),
                pltpu.SemaphoreType.DMA((3,)),
            ],
            compiler_params=pltpu.CompilerParams(
                collective_id=0, has_side_effects=True, vmem_limit_bytes=48 * 2**20
            ),
        )(right_side, offsets, counts)

    part = P(None, "basin", "front", None)
    return jax.shard_map(
        step, mesh=mesh, in_specs=(part, part, P("basin", "front")), out_specs=(part, part), check_vma=False
    )
```

time: 81.3 us -> 55.1 us (0.68)
  Pallas kernels: 77.2 us -> 50.9 us
    pallas_call x1, Pallas kernels: 77.2 us -> 50.9 us  [step(): pl.pallas_call(lambda *refs: kernel(sizes, *refs), out_shape=(shape, shap...]
where the time goes in v2:
time: 55.1 us; the launch traced here: 54.9 us
  Pallas kernels  50.9 us (92%)
  local copies, waits for them, and re-layouts  3.27 us (6%)
  between operations  0.65 us (1%)
    pallas_call x1, Pallas kernels, step(): pl.pallas_call(lambda *refs: kernel(sizes, *refs), out_shape=(shape, shap...  50.9 us
    unnamed x8, local copies, waits for them, and re-layouts  3.27 us

profile of v2, /device:TPU:1, one launch (start us, length us, event | category | flops | bytes accessed | tf_op | source)
XLA Modules:
  0.0 54.9 jit_solution(11421347580354992973)
XLA Ops:
  0.6 0.0 copy-start
  0.6 0.7 %copy-done = f32[4,1,2,512]{3,2,1,0:T(2,128)S(1)} copy-done((f32[4,1,2,512]{3,2,1,0:T(2,128)S(1)}, f32[4,1,2,512]{3,2,1,0:T(2,128)}, u32[]{:S(2)}) %copy-start) | copy-done | bytes 16408
  1.3 0.0 copy-start.1
  1.4 0.7 %copy-done.1 = f32[2,1,2,512]{3,2,1,0:T(2,128)S(1)} copy-done((f32[2,1,2,512]{3,2,1,0:T(2,128)S(1)}, f32[2,1,2,512]{3,2,1,0:T(2,128)}, u32[]{:S(2)}) %copy-start.1) | copy-done | bytes 8216
  2.0 0.0 copy-start.2
  2.0 0.7 %copy-done.2 = s32[1,2]{1,0:T(1,128)S(1)} copy-done((s32[1,2]{1,0:T(1,128)S(1)}, s32[1,2]{1,0:T(1,128)}, u32[]{:S(2)}) %copy-start.2) | copy-done | bytes 32
  2.7 50.9 %shard_map.50 = (f32[4,1,2,512]{3,2,1,0:T(2,128)S(1)}, f32[4,1,2,512]{3,2,1,0:T(2,128)S(1)}) custom-call(f32[4,1,2,512]{3,2,1,0:T(2,128)S(1)} %copy-done, f32[2,1,2,512]{3,2,1,0:T(2,128)S(1)} %copy-done.1, s32[1,2]{1,0:T(1,128)S(1)} %copy-done.2), custom_call_target="tpu_custom_call" | custom-call | tf_op jit(solution)/shard_map/pallas_call | solution.py:379
  53.7 0.6 %copy.7 = f32[4,1,2,512]{3,2,1,0:T(2,128)} copy(f32[4,1,2,512]{3,2,1,0:T(2,128)S(1)} %get-tuple-element.4) | data formatting | bytes 32768
  54.3 0.6 %copy.8 = f32[4,1,2,512]{3,2,1,0:T(2,128)} copy(f32[4,1,2,512]{3,2,1,0:T(2,128)S(1)} %get-tuple-element.5) | data formatting | bytes 32768
Async XLA Ops:
  0.6 0.7 %copy-start = (f32[4,1,2,512]{3,2,1,0:T(2,128)S(1)}, f32[4,1,2,512]{3,2,1,0:T(2,128)}, u32[]{:S(2)}) copy-start(f32[4,1,2,512]{3,2,1,0:T(2,128)} %refs_0_.1) | copy-start | bytes 49156
  1.3 0.7 %copy-start.1 = (f32[2,1,2,512]{3,2,1,0:T(2,128)S(1)}, f32[2,1,2,512]{3,2,1,0:T(2,128)}, u32[]{:S(2)}) copy-start(f32[2,1,2,512]{3,2,1,0:T(2,128)} %refs_1_.1) | copy-start | bytes 24580
  2.0 0.7 %copy-start.2 = (s32[1,2]{1,0:T(1,128)S(1)}, s32[1,2]{1,0:T(1,128)}, u32[]{:S(2)}) copy-start(s32[1,2]{1,0:T(1,128)} %refs_2_.1) | copy-start | bytes 28
